TPU v7x, 512 devices: a whole 4x8x8 slice. The times are simulated.
512 devices in a mesh: chan: 16 (over y_hi, z), ctx: 32 (over y_lo, x, core).
Axes of the slice: x: 4, y: 8 (y_hi: 2, y_lo: 4; y = y_hi * 4 + y_lo), z: 8, core: 2. Of those that a mesh axis runs over, the one named last changes fastest.
Arguments:
- features: float32 [3, 4096, 8192], P(None, 'chan', 'ctx'), may hold values from -6 to 6
- short_conv: float32 [3, 4096, 3], P(None, 'chan'), may hold values from -3 to 3
- filters: float32 [4096, 8192], P('chan', 'ctx'), may hold values from -0.0625 to 0.0625
- skip_gain: float32 [4096], P('chan'), may hold values from 0.5 to 1.5
Outputs:
- mixed: float32 [4096, 8192], P('chan', 'ctx')
All inputs are finite; a program needn't handle non-finite values.
Results may differ from a plain program's by a relative error of at most 0.000064.
Values sent between devices are 32-bit elements; how exact they have to be, the bound alone decides.
A program may use at most 64 MiB of HBM per device.

v0:
```python
import functools

import jax
import jax.numpy as jnp
import numpy as np
from jax import lax
from jax.experimental import pallas as pl
from jax.experimental.pallas import tpu as pltpu
from jax.sharding import PartitionSpec as P

MESH = pl.DeviceIdType.MESH
TILE = 128
PAD = 4
GROUP = 4
LIMIT = 63 * 2**20


def tables(size):
    n, k = np.arange(size)[:, None], np.arange(size)[None, :]
    angle = np.pi * (n * k % (2 * size)) / size
    last = np.where(n % 2 == 0, 1.0, -1.0)
    forward = np.concatenate([np.cos(angle), np.where(k == 0, last, -np.sin(angle))], axis=1)
    weight = np.where(np.arange(size) == 0, 0.5, 1.0) / size
    backward = (forward * np.concatenate([weight, weight])[None, :]).T
    return forward.astype(np.float32), backward.astype(np.float32)


def split(x):
    high = x.astype(jnp.bfloat16)
    return high, (x - high.astype(jnp.float32)).astype(jnp.bfloat16)


def dot3(x, table_high, table_low):
    high, low = split(x)
    dot = functools.partial(jnp.dot, preferred_element_type=jnp.float32)
    return dot(high, table_high[...]) + (dot(low, table_high[...]) + dot(high, table_low[...]))


def kernel(
    n, feat_hbm, taps_hbm, filt_hbm, skip_hbm, forward_hbm, backward_hbm, out_ref,
    feat, filt, taps_ref, skip_ref, forward, backward, fwd_high, fwd_low, bwd_high, bwd_low, rim_out, rim_in, queries, gated, got_f, got_g,
    f_re, f_im, f_sum, g_re, g_im, g_sum, conv_out, conv_in,
    load_sem, rim_send, rim_recv, send_sem, recv_sem,
):
    me = lax.axis_index("ctx")
    channels, tokens = filt.shape
    per = channels // n

    barrier = pltpu.get_barrier_semaphore()

    def greet(step, carry):
        pl.semaphore_signal(barrier, inc=1, device_id={"ctx": lax.rem(me + step, n)}, device_id_type=MESH)
        return carry

    lax.fori_loop(1, n, greet, 0, unroll=True)

    loads = [
        pltpu.make_async_copy(src, dst, load_sem.at[i])
        for i, (src, dst) in enumerate(
            [(feat_hbm, feat), (taps_hbm, taps_ref), (skip_hbm, skip_ref), (filt_hbm, filt), (forward_hbm, forward), (backward_hbm, backward)]
        )
    ]
    for load in loads:
        load.start()

    for load in loads[:3]:
        load.wait()
    scalars = jnp.concatenate(
        [taps_ref[0], taps_ref[1], taps_ref[2], skip_ref[...], jnp.zeros((TILE - 10, channels), jnp.float32)], axis=0
    )
    columns = jnp.transpose(scalars)

    lane = lax.broadcasted_iota(jnp.int32, (channels, TILE), 1)
    ends = [feat[s, :, tokens - TILE :] for s in range(3)]
    merged = jnp.where(
        lane >= TILE - 2,
        ends[2],
        jnp.where(lane >= TILE - 4, pltpu.roll(ends[1], TILE - 2, 1), pltpu.roll(ends[0], TILE - 4, 1)),
    )
    rim_out[...] = jnp.transpose(merged)[TILE - 8 :, :]
    loads[3].wait()

    pl.semaphore_wait(barrier, n - 1)

    rim = pltpu.make_async_remote_copy(
        src_ref=rim_out, dst_ref=rim_in, send_sem=rim_send, recv_sem=rim_recv,
        device_id={"ctx": lax.rem(me + 1, n)}, device_id_type=MESH,
    )
    rim.start()

    def rows(t):
        return pl.ds(pl.multiple_of(t * per, per), per)

    def scatter(source, target, which):
        def send(step, carry):
            t = lax.rem(me + step, n)
            pltpu.make_async_remote_copy(
                src_ref=source.at[rows(t)], dst_ref=target.at[me], send_sem=send_sem.at[which], recv_sem=recv_sem.at[which],
                device_id={"ctx": t}, device_id_type=MESH,
            ).start()
            return carry

        lax.fori_loop(1, n, send, 0, unroll=True)
        pltpu.make_async_copy(source.at[rows(me)], target.at[me], recv_sem.at[which]).start()

    def wait_all(target, which):
        pltpu.make_async_copy(target, target, recv_sem.at[which]).wait()

    scatter(filt, got_f, 0)

    rim.wait()
    rims = jnp.transpose(jnp.concatenate([jnp.zeros((TILE - 8, channels), jnp.float32), rim_in[...]], axis=0))
    rims = jnp.where(me == 0, jnp.zeros_like(rims), rims)

    def featured(s):
        before = [pltpu.roll(rims, 2 * (2 - s) + lag, 1) for lag in (1, 2)]
        taps = [jnp.broadcast_to(columns[:, 3 * s + j : 3 * s + j + 1], (channels, TILE)) for j in range(3)]
        parts = []
        for tile in range(tokens // TILE):
            own = feat[s, :, tile * TILE : (tile + 1) * TILE]
            total = taps[0] * own
            turned = []
            for lag in (1, 2):
                now = pltpu.roll(own, lag, 1)
                total = total + taps[lag] * jnp.where(lane < lag, before[lag - 1], now)
                turned.append(now)
            before = turned
            parts.append(total)
        return parts

    keys, values = featured(1), featured(2)
    for tile in range(tokens // TILE):
        gated[:, tile * TILE : (tile + 1) * TILE] = keys[tile] * values[tile]
    scatter(gated, got_g, 1)
    for tile, part in enumerate(featured(0)):
        queries[:, tile * TILE : (tile + 1) * TILE] = part

    for load in loads[4:]:
        load.wait()
    fwd_high[...], fwd_low[...] = split(forward[...])
    bwd_high[...], bwd_low[...] = split(backward[...])
    wait_all(got_f, 0)
    spectrum = dot3(got_f[...].reshape(channels, tokens), fwd_high, fwd_low)
    real, imag = spectrum[:, :tokens], spectrum[:, tokens:]
    f_re[...] = real.reshape(n, per, tokens)
    f_im[...] = imag.reshape(n, per, tokens)
    f_sum[...] = (real + imag).reshape(n, per, tokens)
    wait_all(got_g, 1)
    spectrum = dot3(got_g[...].reshape(channels, tokens), fwd_high, fwd_low)
    sign = (1 - 2 * (lax.broadcasted_iota(jnp.int32, (1, 1, tokens), 2) % 2)).astype(jnp.float32)
    nothing = jnp.zeros((PAD, per, tokens), jnp.float32)
    sums = []
    for half, store in ((0, g_re), (1, g_im)):
        bins = spectrum[:, half * tokens : (half + 1) * tokens].reshape(n, per, tokens)
        late = jnp.concatenate([nothing[:1], bins[:-1]], axis=0)
        total = bins + sign * late
        store[:PAD] = nothing
        store[PAD:] = total
        sums.append(total)
    g_sum[:PAD] = nothing
    g_sum[PAD:] = sums[0] + sums[1]

    row = 8
    first_lane = lax.broadcasted_iota(jnp.int32, (1, 1, TILE), 2) == 0
    for start in range(0, n, row):
        pieces = {}
        for tile in range(tokens // TILE):
            at = slice(tile * TILE, (tile + 1) * TILE)
            for base in range(start, start + row, GROUP):

                def step(m, acc, base=base, at=at):
                    acc = list(acc)
                    fs = [[ref[GROUP * m + b, :, at] for ref in (f_re, f_im, f_sum)] for b in range(GROUP)]
                    g0 = base - GROUP * m + PAD
                    gs = {d: [ref[g0 + d, :, at] for ref in (g_re, g_im, g_sum)] for d in range(1 - GROUP, GROUP)}
                    for a in range(GROUP):
                        for b in range(GROUP):
                            for part in range(3):
                                acc[3 * a + part] = acc[3 * a + part] + fs[b][part] * gs[a - b][part]
                    return tuple(acc)

                zero = jnp.zeros((per, TILE), jnp.float32)
                acc = lax.fori_loop(0, base // GROUP + 1, step, (zero,) * (3 * GROUP))
                for a in range(GROUP):
                    pieces[tile, base - start + a] = acc[3 * a : 3 * a + 3]
        real_parts, imag_parts = [], []
        for tile in range(tokens // TILE):
            both, cross, mixed_sum = (jnp.concatenate([pieces[tile, a][part] for a in range(row)], axis=0) for part in range(3))
            re, im = both - cross, mixed_sum - both - cross
            if tile == 0:
                packed = lax.broadcasted_iota(jnp.int32, (row * per, TILE), 1) == 0
                re, im = jnp.where(packed, both, re), jnp.where(packed, cross, im)
            real_parts.append(re)
            imag_parts.append(im)
        back = dot3(jnp.concatenate(real_parts + imag_parts, axis=1), bwd_high, bwd_low)
        conv_out[start : start + row] = back.reshape(row, per, tokens)
        for block in range(start, start + row):

            @pl.when(me != block)
            def _(block=block):
                pltpu.make_async_remote_copy(
                    src_ref=conv_out.at[block], dst_ref=conv_in.at[me], send_sem=send_sem.at[2], recv_sem=recv_sem.at[2],
                    device_id={"ctx": block}, device_id_type=MESH,
                ).start()

            @pl.when(me == block)
            def _(block=block):
                pltpu.make_async_copy(conv_out.at[block], conv_in.at[me], recv_sem.at[2]).start()

    wait_all(conv_in, 2)
    skip = jnp.broadcast_to(columns[:, 9:10], (channels, TILE))
    convolved = conv_in[...].reshape(channels, tokens)
    for tile in range(tokens // TILE):
        at = slice(tile * TILE, (tile + 1) * TILE)
        out_ref[:, at] = queries[:, at] * (convolved[:, at] + skip * gated[:, at])
    for which in range(3):
        sent = got_f.at[pl.ds(0, n - 1)]
        pltpu.make_async_copy(sent, sent, send_sem.at[which]).wait()


def solution(mesh):
    n = mesh.shape["ctx"]

    def shards(features, short_conv, filters, skip_gain):
        channels, tokens = filters.shape
        per = channels // n
        any_space, vmem = pl.BlockSpec(memory_space=pl.ANY), pl.BlockSpec(memory_space=pltpu.VMEM)
        real = functools.partial(pltpu.VMEM, dtype=jnp.float32)
        block = (n, per, tokens)
        padded = (n + PAD, per, tokens)
        return pl.pallas_call(
            functools.partial(kernel, n),
            out_shape=jax.ShapeDtypeStruct((channels, tokens), jnp.float32),
            in_specs=[any_space] * 6,
            out_specs=vmem,
            scratch_shapes=[
                real((3, channels, tokens)),
                real((channels, tokens)),
                real((3, 3, channels)),
                real((1, channels)),
                real((tokens, 2 * tokens)),
                real((2 * tokens, tokens)),
                pltpu.VMEM((tokens, 2 * tokens), jnp.bfloat16),
                pltpu.VMEM((tokens, 2 * tokens), jnp.bfloat16),
                pltpu.VMEM((2 * tokens, tokens), jnp.bfloat16),
                pltpu.VMEM((2 * tokens, tokens), jnp.bfloat16),
                real((8, channels)),
                real((8, channels)),
                real((channels, tokens)),
                real((channels, tokens)),
                real(block),
                real(block),
                real(block),
                real(block),
                real(block),
                real(padded),
                real(padded),
                real(padded),
                real(block),
                real(block),
                pltpu.SemaphoreType.DMA((6,)),
                pltpu.SemaphoreType.DMA,
                pltpu.SemaphoreType.DMA,
                pltpu.SemaphoreType.DMA((3,)),
                pltpu.SemaphoreType.DMA((3,)),
            ],
            compiler_params=pltpu.CompilerParams(collective_id=0, has_side_effects=True, vmem_limit_bytes=LIMIT),
        )(features, jnp.transpose(short_conv, (0, 2, 1)), filters, skip_gain.reshape(1, channels), *(jnp.asarray(t) for t in tables(tokens)))

    placed = (P(None, "chan", "ctx"), P(None, "chan", None), P("chan", "ctx"), P("chan"))
    return jax.shard_map(shards, mesh=mesh, in_specs=placed, out_specs=P("chan", "ctx"), check_vma=False)
```

profile of v0, /device:TPU:25, one launch (start us, length us, event | category | flops | bytes accessed | tf_op | source)
XLA Modules:
  0.0 34.7 jit_solution(2919077726597727120)
XLA Ops:
  0.0 33.0 %shard_map.64 = f32[256,256]{1,0:T(8,128)} custom-call(f32[3,256,256]{2,1,0:T(8,128)} %feat_hbm.1, f32[3,3,256]{2,1,0:T(4,128)} %bitcast.2, f32[256,256]{1,0:T(8,128)} %filt_hbm.1, f32[1,256]{1,0:T(1,128)} %bitcast.3, f32[256,512]{1,0:T(8,128)} %constant.4.clone.forward_hbm, f32[512,256]{1,0:T(8,128)} %constant.5.clone.backward_hbm), custom_call_target="tpu_custom_call" | custom-call | tf_op jit(solution)/shard_map/pallas_call | solution.py:231
  33.1 1.7 %copy.8 = f32[256,256]{1,0:T(8,128)} copy(f32[256,256]{1,0:T(8,128)} %shard_map.64) | data formatting | bytes 524288
where the time goes:
time: 34.9 us; the launch traced here: 34.7 us
  Pallas kernels  33 us (95%)
  local copies, waits for them, and re-layouts  1.67 us (5%)
    pallas_call x1, Pallas kernels, shards(): pl.pallas_call(functools.partial(kernel, n), out_shape=jax.ShapeDtypeStru...  33 us
    unnamed x1, local copies, waits for them, and re-layouts  1.67 us

commit v1 on v0

v1 whole, which is shorter than its diff:
```python
import functools

import jax
import jax.numpy as jnp
import numpy as np
from jax import lax
from jax.experimental import pallas as pl
from jax.experimental.pallas import tpu as pltpu
from jax.sharding import PartitionSpec as P

MESH = pl.DeviceIdType.MESH
TILE = 128
PAD = 4
GROUP = 4
LIMIT = 63 * 2**20


def tables(size):
    n, k = np.arange(size)[:, None], np.arange(size)[None, :]
    angle = np.pi * (n * k % (2 * size)) / size
    last = np.where(n % 2 == 0, 1.0, -1.0)
    forward = np.concatenate([np.cos(angle), np.where(k == 0, last, -np.sin(angle))], axis=1)
    weight = np.where(np.arange(size) == 0, 0.5, 1.0) / size
    backward = (forward * np.concatenate([weight, weight])[None, :]).T
    return forward.astype(np.float32), backward.astype(np.float32)


def split(x):
    high = x.astype(jnp.bfloat16)
    return high, (x - high.astype(jnp.float32)).astype(jnp.bfloat16)


def dot3(x, table_high, table_low):
    high, low = split(x)
    dot = functools.partial(jnp.dot, preferred_element_type=jnp.float32)
    return dot(high, table_high[...]) + (dot(low, table_high[...]) + dot(high, table_low[...]))


def swap(first, second):
    half = first.shape[1] // 2
    low = lax.broadcasted_iota(jnp.int32, first.shape, 1) < half
    return jnp.where(low, first, pltpu.roll(second, half, 1)), jnp.where(low, pltpu.roll(first, half, 1), second)


def pairs(blocks):
    split_up = blocks.reshape(blocks.shape[0] // 2, 2, *blocks.shape[1:])
    return swap(split_up[:, 0], split_up[:, 1])


def unpairs(tile0, tile1):
    joined = jnp.stack(swap(tile0, tile1), axis=1)
    return joined.reshape(2 * tile0.shape[0], *tile0.shape[1:])


def kernel(
    n, feat_hbm, taps_hbm, filt_hbm, skip_hbm, forward_hbm, backward_hbm, out_ref,
    feat, filt, taps_ref, skip_ref, forward, backward, fwd_high, fwd_low, bwd_high, bwd_low, rim_out, rim_in, queries, gated, sent_f, sent_g,
    got_f, got_g, f_re, f_im, f_sum, g_re, g_im, g_sum, conv_out, conv_in,
    load_sem, rim_send, rim_recv, send_sem, recv_sem,
):
    me = lax.axis_index("ctx")
    channels, tokens = filt.shape
    per = channels // n
    chunks = 2

    barrier = pltpu.get_barrier_semaphore()

    def greet(step, carry):
        pl.semaphore_signal(barrier, inc=1, device_id={"ctx": lax.rem(me + step, n)}, device_id_type=MESH)
        return carry

    lax.fori_loop(1, n, greet, 0, unroll=True)

    loads = [
        pltpu.make_async_copy(src, dst, load_sem.at[i])
        for i, (src, dst) in enumerate(
            [(feat_hbm, feat), (taps_hbm, taps_ref), (skip_hbm, skip_ref), (filt_hbm, filt), (forward_hbm, forward), (backward_hbm, backward)]
        )
    ]
    for load in loads:
        load.start()
    for load in loads[:3]:
        load.wait()
    scalars = jnp.concatenate(
        [taps_ref[0], taps_ref[1], taps_ref[2], skip_ref[...], jnp.zeros((TILE - 10, channels), jnp.float32)], axis=0
    )
    columns = jnp.transpose(scalars)

    def column(i):
        return jnp.broadcast_to(columns[:, i : i + 1], (channels, TILE))

    lane = lax.broadcasted_iota(jnp.int32, (channels, TILE), 1)
    ends = [feat[s, :, tokens - TILE :] for s in range(3)]
    merged = jnp.where(
        lane >= TILE - 2,
        ends[2],
        jnp.where(lane >= TILE - 4, pltpu.roll(ends[1], TILE - 2, 1), pltpu.roll(ends[0], TILE - 4, 1)),
    )
    rim_out[...] = jnp.transpose(merged)[TILE - 8 :, :]

    def pack(tile0, tile1, target):
        target[0], target[1] = swap(tile0.reshape(n, per, TILE), tile1.reshape(n, per, TILE))

    loads[3].wait()
    pack(filt[:, :TILE], filt[:, TILE:], sent_f)

    pl.semaphore_wait(barrier, n - 1)

    rim = pltpu.make_async_remote_copy(
        src_ref=rim_out, dst_ref=rim_in, send_sem=rim_send, recv_sem=rim_recv,
        device_id={"ctx": lax.rem(me + 1, n)}, device_id_type=MESH,
    )
    rim.start()

    def scatter(source, target, which, chunk):
        def send(step, carry):
            t = lax.rem(me + step, n)
            pltpu.make_async_remote_copy(
                src_ref=source.at[chunk, t], dst_ref=target.at[chunk, me], send_sem=send_sem.at[which, chunk], recv_sem=recv_sem.at[which, chunk],
                device_id={"ctx": t}, device_id_type=MESH,
            ).start()
            return carry

        lax.fori_loop(1, n, send, 0, unroll=True)
        pltpu.make_async_copy(source.at[chunk, me], target.at[chunk, me], recv_sem.at[which, chunk]).start()

    def wait_all(target, which, chunk):
        pltpu.make_async_copy(target.at[chunk], target.at[chunk], recv_sem.at[which, chunk]).wait()

    scatter(sent_f, got_f, 0, 0)
    for load in loads[4:]:
        load.wait()
    fwd_high[...], fwd_low[...] = split(forward[...])
    bwd_high[...], bwd_low[...] = split(backward[...])

    rim.wait()
    rims = jnp.transpose(jnp.concatenate([jnp.zeros((TILE - 8, channels), jnp.float32), rim_in[...]], axis=0))
    rims = jnp.where(me == 0, jnp.zeros_like(rims), rims)

    def featured(s):
        before = [pltpu.roll(rims, 2 * (2 - s) + lag, 1) for lag in (1, 2)]
        taps = [column(3 * s + j) for j in range(3)]
        parts = []
        for tile in range(tokens // TILE):
            own = feat[s, :, tile * TILE : (tile + 1) * TILE]
            total = taps[0] * own
            turned = []
            for lag in (1, 2):
                now = pltpu.roll(own, lag, 1)
                total = total + taps[lag] * jnp.where(lane < lag, before[lag - 1], now)
                turned.append(now)
            before = turned
            parts.append(total)
        return parts

    keys, values = featured(1), featured(2)
    products = [k * v for k, v in zip(keys, values)]
    pack(*products, sent_g)
    scatter(sent_g, got_g, 1, 0)
    scatter(sent_f, got_f, 0, 1)
    scatter(sent_g, got_g, 1, 1)
    skip = column(9)
    for tile, part in enumerate(featured(0)):
        at = slice(tile * TILE, (tile + 1) * TILE)
        queries[:, at] = part
        gated[:, at] = skip * products[tile]

    def spectrum(blocks):
        rows = jnp.concatenate(pairs(blocks), axis=2).reshape(n * per // 2, tokens)
        bins = dot3(rows, fwd_high, fwd_low)
        tiles = [bins[:, i * TILE : (i + 1) * TILE].reshape(n // 2, per, TILE) for i in range(4)]
        return unpairs(tiles[0], tiles[1]), unpairs(tiles[2], tiles[3])

    sign = (1 - 2 * (lax.broadcasted_iota(jnp.int32, (1, 1, TILE), 2) % 2)).astype(jnp.float32)
    nothing = jnp.zeros((PAD, per, TILE), jnp.float32)
    stage_blocks = n // 2

    def filter_spectra(chunk):
        wait_all(got_f, 0, chunk)
        real, imag = spectrum(got_f[chunk])
        f_re[...], f_im[...], f_sum[...] = real, imag, real + imag

    def signal_spectra(chunk):
        wait_all(got_g, 1, chunk)
        sums = []
        for part, store in zip(spectrum(got_g[chunk]), (g_re, g_im)):
            late = jnp.concatenate([nothing[:1], part[:-1]], axis=0)
            total = part + sign * late
            store[:PAD] = nothing
            store[PAD:] = total
            sums.append(total)
        g_sum[:PAD] = nothing
        g_sum[PAD:] = sums[0] + sums[1]

    def convolve(chunk):
        for stage in range(2):
            start = stage_blocks * lax.rem(me // stage_blocks + 1 + stage, 2)
            pieces = []
            for first in range(0, stage_blocks, GROUP):
                base = start + first

                def step(m, acc, base=base):
                    acc = list(acc)
                    fs = [[ref[GROUP * m + b] for ref in (f_re, f_im, f_sum)] for b in range(GROUP)]
                    g0 = base - GROUP * m + PAD
                    gs = {d: [ref[g0 + d] for ref in (g_re, g_im, g_sum)] for d in range(1 - GROUP, GROUP)}
                    for a in range(GROUP):
                        for b in range(GROUP):
                            for part in range(3):
                                acc[3 * a + part] = acc[3 * a + part] + fs[b][part] * gs[a - b][part]
                    return tuple(acc)

                zero = jnp.zeros((per, TILE), jnp.float32)
                acc = lax.fori_loop(0, base // GROUP + 1, step, (zero,) * (3 * GROUP))
                pieces += [acc[3 * a : 3 * a + 3] for a in range(GROUP)]
            both, cross, total = (jnp.stack([piece[part] for piece in pieces], axis=0) for part in range(3))
            real, imag = both - cross, total - both - cross
            packed = (lax.broadcasted_iota(jnp.int32, real.shape, 2) == 0) & (lax.broadcasted_iota(jnp.int32, real.shape, 1) < per // 2)
            real, imag = jnp.where(packed, both, real), jnp.where(packed, cross, imag)
            rows = jnp.concatenate([*pairs(real), *pairs(imag)], axis=2).reshape(stage_blocks * per // 2, 2 * tokens)
            back = dot3(rows, bwd_high, bwd_low)
            tiles = [back[:, i * TILE : (i + 1) * TILE].reshape(stage_blocks // 2, per, TILE) for i in range(2)]
            conv_out[chunk, pl.ds(start, stage_blocks)] = unpairs(*tiles)

            def send(i, carry, start=start):
                t = start + lax.rem(me + i, stage_blocks)
                pltpu.make_async_remote_copy(
                    src_ref=conv_out.at[chunk, t], dst_ref=conv_in.at[chunk, me], send_sem=send_sem.at[2, chunk], recv_sem=recv_sem.at[2, chunk],
                    device_id={"ctx": t}, device_id_type=MESH,
                ).start()
                return carry

            lax.fori_loop(stage, stage_blocks, send, 0, unroll=True)
        pltpu.make_async_copy(conv_out.at[chunk, me], conv_in.at[chunk, me], recv_sem.at[2, chunk]).start()

    for chunk in range(chunks):
        filter_spectra(chunk)
        signal_spectra(chunk)
        convolve(chunk)

    for chunk in range(chunks):
        wait_all(conv_in, 2, chunk)
    for tile, part in enumerate(swap(conv_in[0], conv_in[1])):
        at = slice(tile * TILE, (tile + 1) * TILE)
        out_ref[:, at] = queries[:, at] * (part.reshape(channels, TILE) + gated[:, at])
    for which in range(3):
        for chunk in range(chunks):
            sent = got_f.at[chunk, pl.ds(0, n - 1)]
            pltpu.make_async_copy(sent, sent, send_sem.at[which, chunk]).wait()


def solution(mesh):
    n = mesh.shape["ctx"]

    def shards(features, short_conv, filters, skip_gain):
        channels, tokens = filters.shape
        per = channels // n
        any_space, vmem = pl.BlockSpec(memory_space=pl.ANY), pl.BlockSpec(memory_space=pltpu.VMEM)
        real = functools.partial(pltpu.VMEM, dtype=jnp.float32)
        moved, spectra, padded = (2, n, per, TILE), (n, per, TILE), (n + PAD, per, TILE)
        return pl.pallas_call(
            functools.partial(kernel, n),
            out_shape=jax.ShapeDtypeStruct((channels, tokens), jnp.float32),
            in_specs=[any_space] * 6,
            out_specs=vmem,
            scratch_shapes=[
                real((3, channels, tokens)),
                real((channels, tokens)),
                real((3, 3, channels)),
                real((1, channels)),
                real((tokens, 2 * tokens)),
                real((2 * tokens, tokens)),
                pltpu.VMEM((tokens, 2 * tokens), jnp.bfloat16),
                pltpu.VMEM((tokens, 2 * tokens), jnp.bfloat16),
                pltpu.VMEM((2 * tokens, tokens), jnp.bfloat16),
                pltpu.VMEM((2 * tokens, tokens), jnp.bfloat16),
                real((8, channels)),
                real((8, channels)),
                real((channels, tokens)),
                real((channels, tokens)),
                real(moved),
                real(moved),
                real(moved),
                real(moved),
                real(spectra),
                real(spectra),
                real(spectra),
                real(padded),
                real(padded),
                real(padded),
                real(moved),
                real(moved),
                pltpu.SemaphoreType.DMA((6,)),
                pltpu.SemaphoreType.DMA,
                pltpu.SemaphoreType.DMA,
                pltpu.SemaphoreType.DMA((3, 2)),
                pltpu.SemaphoreType.DMA((3, 2)),
            ],
            compiler_params=pltpu.CompilerParams(collective_id=0, has_side_effects=True, vmem_limit_bytes=LIMIT),
        )(features, jnp.transpose(short_conv, (0, 2, 1)), filters, skip_gain.reshape(1, channels), *(jnp.asarray(t) for t in tables(tokens)))

    placed = (P(None, "chan", "ctx"), P(None, "chan", None), P("chan", "ctx"), P("chan"))
    return jax.shard_map(shards, mesh=mesh, in_specs=placed, out_specs=P("chan", "ctx"), check_vma=False)
```

time: 34.9 us -> 33 us (0.946)
  the two profiles are of different devices: /device:TPU:25 before, /device:TPU:1 now
where the time goes in v1:
time: 33 us; the launch traced here: 32.8 us
  Pallas kernels  31.2 us (95%)
  local copies, waits for them, and re-layouts  1.67 us (5%)
    pallas_call x1, Pallas kernels, shards(): pl.pallas_call(functools.partial(kernel, n), out_shape=jax.ShapeDtypeStru...  31.2 us
    unnamed x1, local copies, waits for them, and re-layouts  1.67 us

profile of v1, /device:TPU:1, one launch (start us, length us, event | category | flops | bytes accessed | tf_op | source)
XLA Modules:
  0.0 32.8 jit_solution(4875711959190864622)
XLA Ops:
  0.0 31.2 %shard_map.64 = f32[256,256]{1,0:T(8,128)} custom-call(f32[3,256,256]{2,1,0:T(8,128)} %feat_hbm.1, f32[3,3,256]{2,1,0:T(4,128)} %bitcast.2, f32[256,256]{1,0:T(8,128)} %filt_hbm.1, f32[1,256]{1,0:T(1,128)} %bitcast.3, f32[256,512]{1,0:T(8,128)} %constant.4.clone.forward_hbm, f32[512,256]{1,0:T(8,128)} %constant.5.clone.backward_hbm), custom_call_target="tpu_custom_call" | custom-call | tf_op jit(solution)/shard_map/pallas_call | solution.py:261
  31.2 1.7 %copy.8 = f32[256,256]{1,0:T(8,128)} copy(f32[256,256]{1,0:T(8,128)} %shard_map.64) | data formatting | bytes 524288

commit v2 on v1

--- a/solution.py
+++ b/solution.py
@@ -53,10 +53,10 @@
 
 
 def kernel(
-    n, feat_hbm, taps_hbm, filt_hbm, skip_hbm, forward_hbm, backward_hbm, out_ref,
+    n, feat_hbm, taps_hbm, filt_hbm, skip_hbm, forward_hbm, backward_hbm, conv_in, queries_out, gated_out,
     feat, filt, taps_ref, skip_ref, forward, backward, fwd_high, fwd_low, bwd_high, bwd_low, rim_out, rim_in, queries, gated, sent_f, sent_g,
-    got_f, got_g, f_re, f_im, f_sum, g_re, g_im, g_sum, conv_out, conv_in,
-    load_sem, rim_send, rim_recv, send_sem, recv_sem,
+    got_f, got_g, f_re, f_im, f_sum, g_re, g_im, g_sum, conv_out,
+    load_sem, store_sem, rim_send, rim_recv, send_sem, recv_sem,
 ):
     me = lax.axis_index("ctx")
     channels, tokens = filt.shape
@@ -164,12 +164,23 @@
         at = slice(tile * TILE, (tile + 1) * TILE)
         queries[:, at] = part
         gated[:, at] = skip * products[tile]
+    stores = [
+        pltpu.make_async_copy(src, dst, store_sem.at[i]) for i, (src, dst) in enumerate([(queries, queries_out), (gated, gated_out)])
+    ]
+    for store in stores:
+        store.start()
 
     def spectrum(blocks):
         rows = jnp.concatenate(pairs(blocks), axis=2).reshape(n * per // 2, tokens)
         bins = dot3(rows, fwd_high, fwd_low)
         tiles = [bins[:, i * TILE : (i + 1) * TILE].reshape(n // 2, per, TILE) for i in range(4)]
         return unpairs(tiles[0], tiles[1]), unpairs(tiles[2], tiles[3])
+
+    turned = lax.axis_index("chan") // (lax.axis_size("chan") // 2)
+
+    def turn(i, blocks):
+        row = blocks // 2
+        return row * (turned + (1 - 2 * turned) * (i // row)) + lax.rem(i, row)
 
     sign = (1 - 2 * (lax.broadcasted_iota(jnp.int32, (1, 1, TILE), 2) % 2)).astype(jnp.float32)
     nothing = jnp.zeros((PAD, per, TILE), jnp.float32)
@@ -223,14 +234,17 @@
             conv_out[chunk, pl.ds(start, stage_blocks)] = unpairs(*tiles)
 
             def send(i, carry, start=start):
-                t = start + lax.rem(me + i, stage_blocks)
-                pltpu.make_async_remote_copy(
-                    src_ref=conv_out.at[chunk, t], dst_ref=conv_in.at[chunk, me], send_sem=send_sem.at[2, chunk], recv_sem=recv_sem.at[2, chunk],
-                    device_id={"ctx": t}, device_id_type=MESH,
-                ).start()
+                t = start + (turn(i, stage_blocks) if chunk == chunks - 1 else lax.rem(me + i, stage_blocks))
+                @pl.when(t != me)
+                def _():
+                    pltpu.make_async_remote_copy(
+                        src_ref=conv_out.at[chunk, t], dst_ref=conv_in.at[chunk, me], send_sem=send_sem.at[2, chunk], recv_sem=recv_sem.at[2, chunk],
+                        device_id={"ctx": t}, device_id_type=MESH,
+                    ).start()
+
                 return carry
 
-            lax.fori_loop(stage, stage_blocks, send, 0, unroll=True)
+            lax.fori_loop(0, stage_blocks, send, 0, unroll=True)
         pltpu.make_async_copy(conv_out.at[chunk, me], conv_in.at[chunk, me], recv_sem.at[2, chunk]).start()
 
     for chunk in range(chunks):
@@ -240,13 +254,35 @@
 
     for chunk in range(chunks):
         wait_all(conv_in, 2, chunk)
-    for tile, part in enumerate(swap(conv_in[0], conv_in[1])):
-        at = slice(tile * TILE, (tile + 1) * TILE)
-        out_ref[:, at] = queries[:, at] * (part.reshape(channels, TILE) + gated[:, at])
     for which in range(3):
         for chunk in range(chunks):
             sent = got_f.at[chunk, pl.ds(0, n - 1)]
             pltpu.make_async_copy(sent, sent, send_sem.at[which, chunk]).wait()
+    for store in stores:
+        store.wait()
+
+
+def finish(conv_hbm, queries_hbm, gated_hbm, out_hbm, conv, queries, gated, out, load_sem, store_sem):
+    parts = load_sem.shape[1]
+    n, per = conv.shape[1:3]
+    loads, stores = [], []
+    for i in range(parts):
+        blocks, rows = pl.ds(i * n // parts, n // parts), pl.ds(i * n * per // parts, n * per // parts)
+        views = [(conv_hbm.at[:, blocks], conv.at[:, blocks]), (queries_hbm.at[rows], queries.at[rows]), (gated_hbm.at[rows], gated.at[rows])]
+        loads.append([pltpu.make_async_copy(src, dst, load_sem.at[j, i]) for j, (src, dst) in enumerate(views)])
+        stores.append(pltpu.make_async_copy(out.at[rows], out_hbm.at[rows], store_sem.at[i]))
+        for load in loads[-1]:
+            load.start()
+    for i in range(parts):
+        blocks, rows = pl.ds(i * n // parts, n // parts), pl.ds(i * n * per // parts, n * per // parts)
+        for load in loads[i]:
+            load.wait()
+        for tile, part in enumerate(swap(conv[0, blocks], conv[1, blocks])):
+            at = slice(tile * TILE, (tile + 1) * TILE)
+            out[rows, at] = queries[rows, at] * (part.reshape(n * per // parts, TILE) + gated[rows, at])
+        stores[i].start()
+    for store in stores:
+        store.wait()
 
 
 def solution(mesh):
@@ -255,14 +291,15 @@
     def shards(features, short_conv, filters, skip_gain):
         channels, tokens = filters.shape
         per = channels // n
-        any_space, vmem = pl.BlockSpec(memory_space=pl.ANY), pl.BlockSpec(memory_space=pltpu.VMEM)
+        any_space = pl.BlockSpec(memory_space=pl.ANY)
         real = functools.partial(pltpu.VMEM, dtype=jnp.float32)
         moved, spectra, padded = (2, n, per, TILE), (n, per, TILE), (n + PAD, per, TILE)
-        return pl.pallas_call(
+        whole = jax.ShapeDtypeStruct((channels, tokens), jnp.float32)
+        arrived = pl.pallas_call(
             functools.partial(kernel, n),
-            out_shape=jax.ShapeDtypeStruct((channels, tokens), jnp.float32),
+            out_shape=(jax.ShapeDtypeStruct(moved, jnp.float32), whole, whole),
             in_specs=[any_space] * 6,
-            out_specs=vmem,
+            out_specs=(any_space,) * 3,
             scratch_shapes=[
                 real((3, channels, tokens)),
                 real((channels, tokens)),
@@ -289,8 +326,8 @@
                 real(padded),
                 real(padded),
                 real(moved),
-                real(moved),
                 pltpu.SemaphoreType.DMA((6,)),
+                pltpu.SemaphoreType.DMA((2,)),
                 pltpu.SemaphoreType.DMA,
                 pltpu.SemaphoreType.DMA,
                 pltpu.SemaphoreType.DMA((3, 2)),
@@ -298,6 +335,22 @@
             ],
             compiler_params=pltpu.CompilerParams(collective_id=0, has_side_effects=True, vmem_limit_bytes=LIMIT),
         )(features, jnp.transpose(short_conv, (0, 2, 1)), filters, skip_gain.reshape(1, channels), *(jnp.asarray(t) for t in tables(tokens)))
+        parts = 1
+        return pl.pallas_call(
+            finish,
+            out_shape=whole,
+            in_specs=[any_space] * 3,
+            out_specs=any_space,
+            scratch_shapes=[
+                real(moved),
+                real((channels, tokens)),
+                real((channels, tokens)),
+                real((channels, tokens)),
+                pltpu.SemaphoreType.DMA((3, parts)),
+                pltpu.SemaphoreType.DMA((parts,)),
+            ],
+            compiler_params=pltpu.CompilerParams(vmem_limit_bytes=LIMIT),
+        )(*arrived)
 
     placed = (P(None, "chan", "ctx"), P(None, "chan", None), P("chan", "ctx"), P("chan"))
     return jax.shard_map(shards, mesh=mesh, in_specs=placed, out_specs=P("chan", "ctx"), check_vma=False)

time: 33 us -> 32.2 us (0.976)
  local copies, waits for them, and re-layouts: 1.67 us -> 0 us
  Pallas kernels: 31.2 us -> 32 us
    unnamed x1 -> x0, local copies, waits for them, and re-layouts: 1.67 us -> none
    pallas_call x1 -> x2, Pallas kernels: 31.2 us -> 32 us  [the longest x1 30.1 us: shards(): pl.pallas_call(functools.partial(kernel, n), out_shape=(jax.ShapeDtypeStr...]
where the time goes in v2:
time: 32.2 us; the launch traced here: 32 us
  Pallas kernels  32 us (99%)
    pallas_call x1, Pallas kernels, shards(): pl.pallas_call(functools.partial(kernel, n), out_shape=(jax.ShapeDtypeStr...  30.1 us
    pallas_call x1, Pallas kernels, shards(): pl.pallas_call(finish, out_shape=whole, in_specs=[any_space] * 3, out_spe...  1.89 us

profile of v2, /device:TPU:1, one launch (start us, length us, event | category | flops | bytes accessed | tf_op | source)
XLA Modules:
  0.0 32.0 jit_solution(5881353192985416300)
XLA Ops:
  0.0 30.1 %shard_map.64 = (f32[2,32,8,128]{3,2,1,0:T(8,128)}, f32[256,256]{1,0:T(8,128)}, f32[256,256]{1,0:T(8,128)}) custom-call(f32[3,256,256]{2,1,0:T(8,128)} %feat_hbm.1, f32[3,3,256]{2,1,0:T(4,128)} %bitcast.2, f32[256,256]{1,0:T(8,128)} %filt_hbm.1, f32[1,256]{1,0:T(1,128)} %bitcast.3, f32[256,512]{1,0:T(8,128)} %constant.4.clone.forward_hbm, ...), custom_call_target="tpu_custom_call" | custom-call | tf_op jit(solution)/shard_map/pallas_call | solution.py:298
  30.1 1.9 %shard_map.65 = f32[256,256]{1,0:T(8,128)} custom-call(f32[2,32,8,128]{3,2,1,0:T(8,128)} %get-tuple-element.8.conv_hbm, f32[256,256]{1,0:T(8,128)} %get-tuple-element.9.queries_hbm, f32[256,256]{1,0:T(8,128)} %get-tuple-element.10.gated_hbm), custom_call_target="tpu_custom_call" | custom-call | tf_op jit(solution)/shard_map/pallas_call | solution.py:339

commit v3 on v2

--- a/solution.py
+++ b/solution.py
@@ -204,10 +204,13 @@
         g_sum[PAD:] = sums[0] + sums[1]
 
     def convolve(chunk):
-        for stage in range(2):
-            start = stage_blocks * lax.rem(me // stage_blocks + 1 + stage, 2)
+        row = stage_blocks // 2
+        for stage, blocks in ([(0, row), (1, row), (2, stage_blocks)] if chunk == chunks - 1 else [(0, stage_blocks), (2, stage_blocks)]):
+            start = stage_blocks * lax.rem(me // stage_blocks + 1 + stage // 2, 2)
+            if blocks == row:
+                start = start + row * lax.rem(turned + stage, 2)
             pieces = []
-            for first in range(0, stage_blocks, GROUP):
+            for first in range(0, blocks, GROUP):
                 base = start + first
 
                 def step(m, acc, base=base):
@@ -228,13 +231,17 @@
             real, imag = both - cross, total - both - cross
             packed = (lax.broadcasted_iota(jnp.int32, real.shape, 2) == 0) & (lax.broadcasted_iota(jnp.int32, real.shape, 1) < per // 2)
             real, imag = jnp.where(packed, both, real), jnp.where(packed, cross, imag)
-            rows = jnp.concatenate([*pairs(real), *pairs(imag)], axis=2).reshape(stage_blocks * per // 2, 2 * tokens)
+            rows = jnp.concatenate([*pairs(real), *pairs(imag)], axis=2).reshape(blocks * per // 2, 2 * tokens)
             back = dot3(rows, bwd_high, bwd_low)
-            tiles = [back[:, i * TILE : (i + 1) * TILE].reshape(stage_blocks // 2, per, TILE) for i in range(2)]
-            conv_out[chunk, pl.ds(start, stage_blocks)] = unpairs(*tiles)
-
-            def send(i, carry, start=start):
-                t = start + (turn(i, stage_blocks) if chunk == chunks - 1 else lax.rem(me + i, stage_blocks))
+            tiles = [back[:, i * TILE : (i + 1) * TILE].reshape(blocks // 2, per, TILE) for i in range(2)]
+            conv_out[chunk, pl.ds(start, blocks)] = unpairs(*tiles)
+
+            def send(i, carry, start=start, blocks=blocks):
+                if chunk < chunks - 1:
+                    t = start + lax.rem(me + i, blocks)
+                else:
+                    t = start + (i if blocks == row else turn(i, blocks))
+
                 @pl.when(t != me)
                 def _():
                     pltpu.make_async_remote_copy(
@@ -244,7 +251,7 @@
 
                 return carry
 
-            lax.fori_loop(0, stage_blocks, send, 0, unroll=True)
+            lax.fori_loop(0, blocks, send, 0, unroll=True)
         pltpu.make_async_copy(conv_out.at[chunk, me], conv_in.at[chunk, me], recv_sem.at[2, chunk]).start()
 
     for chunk in range(chunks):

time: 32.2 us -> 32.3 us (level)
  no operation moved by 1% of the time
where the time goes in v3:
time: 32.3 us; the launch traced here: 32.1 us
  Pallas kernels  32.1 us (99%)
    pallas_call x1, Pallas kernels, shards(): pl.pallas_call(functools.partial(kernel, n), out_shape=(jax.ShapeDtypeStr...  30.2 us
    pallas_call x1, Pallas kernels, shards(): pl.pallas_call(finish, out_shape=whole, in_specs=[any_space] * 3, out_spe...  1.89 us

profile of v3, /device:TPU:1, one launch (start us, length us, event | category | flops | bytes accessed | tf_op | source)
XLA Modules:
  0.0 32.1 jit_solution(16020458793907440131)
XLA Ops:
  0.0 30.2 %shard_map.64 = (f32[2,32,8,128]{3,2,1,0:T(8,128)}, f32[256,256]{1,0:T(8,128)}, f32[256,256]{1,0:T(8,128)}) custom-call(f32[3,256,256]{2,1,0:T(8,128)} %feat_hbm.1, f32[3,3,256]{2,1,0:T(4,128)} %bitcast.2, f32[256,256]{1,0:T(8,128)} %filt_hbm.1, f32[1,256]{1,0:T(1,128)} %bitcast.3, f32[256,512]{1,0:T(8,128)} %constant.4.clone.forward_hbm, ...), custom_call_target="tpu_custom_call" | custom-call | tf_op jit(solution)/shard_map/pallas_call | solution.py:305
  30.2 1.9 %shard_map.65 = f32[256,256]{1,0:T(8,128)} custom-call(f32[2,32,8,128]{3,2,1,0:T(8,128)} %get-tuple-element.8.conv_hbm, f32[256,256]{1,0:T(8,128)} %get-tuple-element.9.queries_hbm, f32[256,256]{1,0:T(8,128)} %get-tuple-element.10.gated_hbm), custom_call_target="tpu_custom_call" | custom-call | tf_op jit(solution)/shard_map/pallas_call | solution.py:346
